TPU v7x, 128 devices: a whole 4x4x4 slice. The times are simulated.
128 devices in a mesh: pb: 16 (over z, y), ka: 8 (over x, core).
Axes of the slice: x: 4, y: 4, z: 4, core: 2. Of those that a mesh axis runs over, the one named last changes fastest.
Arguments:
- queries: bfloat16 [16384, 256], P('pb'), may hold values from -4.5 to 4.5
- keys: bfloat16 [16384, 256], P('ka'), may hold values from -4.5 to 4.5
- values: bfloat16 [16384, 256], P('ka'), may hold values from -6 to 6
- grad_out: bfloat16 [16384, 256], P('pb'), may hold values from -384 to 384
- key_lengths: int32 [8], P('ka'), may hold values from 1024 to 2048, as said below
Outputs:
- grad_queries: float32 [16384, 256], P(('pb', 'ka'))
- grad_keys: float32 [16384, 256], P(('ka', 'pb'))
- grad_values: float32 [16384, 256], P(('ka', 'pb'))
Inputs may be any that keep to these rules, and one draw needn't show every extreme that they name: Key block b holds key_lengths[b] valid keys at its start, the rest are padding.
All inputs are finite; a program needn't handle non-finite values.
Results may differ from a plain program's by a relative error of at most 0.0035.
Values sent between devices are 32-bit elements; how exact they have to be, the bound alone decides.
A program may use at most 64 MiB of HBM per device.

v0:
```python
import jax
import jax.numpy as jnp
from jax import lax
from jax.sharding import PartitionSpec as P

HD = 128


relax_weight = 0.9


def row_merge(peaks, masses):
    highest = lax.pmax(peaks, "ka")
    return (highest, lax.psum(masses * jnp.exp(peaks - highest), "ka"))


def col_merge(peaks, masses):
    highest = lax.pmax(peaks, "pb")
    return (highest, lax.psum(masses * jnp.exp(peaks - highest), "pb"))


def row_total(partial_sum):
    return lax.psum(partial_sum, "ka")


def col_total(partial_sum):
    return lax.psum(partial_sum, "pb")


def shards(queries, keys, values, grad_out, key_lengths):
    row_count, feature_width = queries.shape
    col_count = keys.shape[0]
    head_count = feature_width // HD
    scaling = HD ** (-0.5)
    block_rows = min(512, row_count)
    block_count = row_count // block_rows
    query_blocks = queries.reshape(block_count, block_rows, head_count, HD)
    grad_blocks = grad_out.reshape(block_count, block_rows, head_count, HD)
    key_heads = keys.reshape(col_count, head_count, HD)
    value_heads = values.reshape(col_count, head_count, HD)
    is_valid = jnp.arange(col_count, dtype=jnp.int32) < key_lengths[0]

    def scores(query_block):
        return (
            jnp.einsum("bhd,khd->hbk", query_block, key_heads, preferred_element_type=jnp.float32)
            * scaling
        )

    def masked_exp(logits):
        return jnp.where(is_valid, jnp.exp(logits), 0.0)

    def to_blocks(vector):
        return vector.reshape(head_count, block_count, block_rows).transpose(1, 0, 2)

    def from_blocks(stacked):
        return stacked.transpose(1, 0, 2).reshape(head_count, row_count)

    def row_potential(col_pot):

        def row_one_block(query_block):
            logits = jnp.where(is_valid, scores(query_block) + col_pot[:, None, :], -jnp.inf)
            peak = jnp.max(logits, axis=-1)
            return (peak, jnp.sum(jnp.exp(logits - peak[..., None]), axis=-1))

        peaks, masses = lax.map(row_one_block, query_blocks)
        highest, mass = row_merge(from_blocks(peaks), from_blocks(masses))
        return -(highest + jnp.log(mass))

    def col_potential(row_pot):

        def col_one_block(inputs):
            query_block, pot_block = inputs
            logits = scores(query_block) + pot_block[:, :, None]
            peak = jnp.max(logits, axis=1)
            return (peak, jnp.sum(jnp.exp(logits - peak[:, None, :]), axis=1))

        peaks, masses = lax.map(col_one_block, (query_blocks, to_blocks(row_pot)))
        highest = jnp.max(peaks, axis=0)
        mass = jnp.sum(masses * jnp.exp(peaks - highest), axis=0)
        highest, mass = col_merge(highest, mass)
        return -relax_weight * (highest + jnp.log(mass))

    zero_cols = jnp.zeros((head_count, col_count), jnp.float32)
    row_first = row_potential(zero_cols)
    col_first = col_potential(row_first)
    row_second = row_potential(col_first)
    col_second = col_potential(row_second)

    def first_pass(carry, inputs):
        col_acc, value_acc = carry
        query_block, grad_block, pot_block = inputs
        logits = scores(query_block)
        probs = masked_exp(logits + pot_block[:, :, None] + col_second[:, None, :])
        grad_probs = jnp.einsum(
            "bhd,khd->hbk", grad_block, value_heads, preferred_element_type=jnp.float32
        )
        product = probs * grad_probs
        value_acc = value_acc + jnp.einsum(
            "hbk,bhd->khd",
            probs.astype(jnp.bfloat16),
            grad_block,
            preferred_element_type=jnp.float32,
        )
        return ((col_acc + jnp.sum(product, axis=1), value_acc), jnp.sum(product, axis=-1))

    init_grads = jnp.zeros((col_count, head_count, HD), jnp.float32)
    (col_part, value_acc), row_parts = lax.scan(
        first_pass, (zero_cols, init_grads), (query_blocks, grad_blocks, to_blocks(row_second))
    )
    value_grad = value_acc.reshape(col_count, feature_width)
    col_adjoint = col_total(col_part)
    row_adjoint = from_blocks(row_parts)

    def second_pass(inputs):
        query_block, pot_block = inputs
        weights = masked_exp(
            scores(query_block) + pot_block[:, :, None] + col_second[:, None, :] / relax_weight
        )
        return jnp.sum(weights * col_adjoint[:, None, :], axis=-1)

    coupled = from_blocks(lax.map(second_pass, (query_blocks, to_blocks(row_second))))
    row_second_adj = row_total(row_adjoint) - relax_weight * row_total(coupled)

    def third_pass(inputs):
        query_block, adj_block, pot_block = inputs
        weights = masked_exp(scores(query_block) + col_first[:, None, :] + pot_block[:, :, None])
        return -jnp.sum(weights * adj_block[:, :, None], axis=1)

    col_first_adj = col_total(
        jnp.sum(
            lax.map(third_pass, (query_blocks, to_blocks(row_second_adj), to_blocks(row_second))),
            axis=0,
        )
    )

    def fourth_pass(inputs):
        query_block, pot_block = inputs
        weights = masked_exp(
            scores(query_block) + pot_block[:, :, None] + col_first[:, None, :] / relax_weight
        )
        return -relax_weight * jnp.sum(weights * col_first_adj[:, None, :], axis=-1)

    row_first_adj = row_total(
        from_blocks(lax.map(fourth_pass, (query_blocks, to_blocks(row_first))))
    )

    def fifth_pass(key_acc, inputs):
        query_block, grad_block, first_block, second_block, second_adj, first_adj = inputs
        logits = scores(query_block)
        probs = masked_exp(logits + second_block[:, :, None] + col_second[:, None, :])
        grad_probs = jnp.einsum(
            "bhd,khd->hbk", grad_block, value_heads, preferred_element_type=jnp.float32
        )
        grad_logits = probs * grad_probs
        grad_logits = grad_logits - relax_weight * col_adjoint[:, None, :] * masked_exp(
            logits + second_block[:, :, None] + col_second[:, None, :] / relax_weight
        )
        grad_logits = grad_logits - second_adj[:, :, None] * masked_exp(
            logits + col_first[:, None, :] + second_block[:, :, None]
        )
        grad_logits = grad_logits - relax_weight * col_first_adj[:, None, :] * masked_exp(
            logits + first_block[:, :, None] + col_first[:, None, :] / relax_weight
        )
        grad_logits = grad_logits - first_adj[:, :, None] * masked_exp(
            logits + first_block[:, :, None]
        )
        rounded_logits = grad_logits.astype(jnp.bfloat16)
        query_grad = (
            jnp.einsum(
                "hbk,khd->bhd", rounded_logits, key_heads, preferred_element_type=jnp.float32
            )
            * scaling
        )
        key_acc = (
            key_acc
            + jnp.einsum(
                "hbk,bhd->khd", rounded_logits, query_block, preferred_element_type=jnp.float32
            )
            * scaling
        )
        return (key_acc, query_grad)

    key_acc, query_parts = lax.scan(
        fifth_pass,
        init_grads,
        (
            query_blocks,
            grad_blocks,
            to_blocks(row_first),
            to_blocks(row_second),
            to_blocks(row_second_adj),
            to_blocks(row_first_adj),
        ),
    )
    query_grad = query_parts.reshape(row_count, feature_width)
    query_shard = lax.psum_scatter(query_grad, "ka", scatter_dimension=0, tiled=True)
    key_grad = key_acc.reshape(col_count, feature_width)
    key_shard, value_shard = (
        lax.psum_scatter(key_grad, "pb", scatter_dimension=0, tiled=True),
        lax.psum_scatter(value_grad, "pb", scatter_dimension=0, tiled=True),
    )
    return (query_shard, key_shard, value_shard)


def solution(mesh):
    placed = (P("pb", None), P("ka", None), P("ka", None), P("pb", None), P("ka"))
    return jax.shard_map(
        shards,
        mesh=mesh,
        in_specs=placed,
        out_specs=(P(("pb", "ka"), None), P(("ka", "pb"), None), P(("ka", "pb"), None)),
        check_vma=False,
    )
```

profile of v0, /device:TPU:0, one launch (start us, length us, event | category | flops | bytes accessed | tf_op | source)
XLA Modules:
  0.0 837.2 jit_solution(11289982290909978880)
XLA Ops:
  7.2 1.5 copy.15
  10.7 8.0 while.113
  11.4 1.4 fusion.132
  12.8 1.9 exponential_reduce_fusion.10
  15.4 1.4 fusion.132
  16.8 1.9 exponential_reduce_fusion.10
  18.7 14.9 %pmax.28 = f32[2,1024]{1,0:T(2,128)S(1)} all-reduce(f32[2,1024]{1,0:T(2,128)S(1)} %bitcast.259), channel_id=1, replica_groups=mesh['pb'=16,'ka'=8] {'ka'}, use_global_device_ids=true, to_apply=%region_4.5 | all-reduce | flops 2048 | bytes 16384 | tf_op jit(solution)/shard_map/pmax | solution.py:13
  33.7 12.7 %psum.63 = f32[2,1024]{1,0:T(2,128)S(1)} all-reduce(f32[2,1024]{1,0:T(2,128)S(1)} %exponential_multiply_fusion.3), channel_id=1, replica_groups=mesh['pb'=16,'ka'=8] {'ka'}, use_global_device_ids=true, to_apply=%region_5.6 | all-reduce | flops 2048 | bytes 16384 | tf_op jit(solution)/shard_map/psum | solution.py:14
  46.4 6.3 while.111
  46.4 1.3 fusion.128
  47.7 1.8 exponential_reduce_fusion.8
  49.6 1.3 fusion.128
  50.9 1.8 exponential_reduce_fusion.8
  52.8 75.9 %pmax.29 = f32[2,2048]{1,0:T(2,128)S(1)} all-reduce(f32[2,2048]{1,0:T(2,128)S(1)} %reduce_max.54), channel_id=1, replica_groups=mesh['pb'=16,'ka'=8] {'pb'}, use_global_device_ids=true, to_apply=%region_11.12 | all-reduce | flops 4096 | bytes 32768 | tf_op jit(solution)/shard_map/pmax | solution.py:18
  128.8 69.5 %psum.64 = f32[2,2048]{1,0:T(2,128)S(1)} all-reduce(f32[2,2048]{1,0:T(2,128)S(1)} %exponential_multiply_fusion.1), channel_id=1, replica_groups=mesh['pb'=16,'ka'=8] {'pb'}, use_global_device_ids=true, to_apply=%region_13.14 | all-reduce | flops 4096 | bytes 32768 | tf_op jit(solution)/shard_map/psum | solution.py:19
  198.3 8.5 %while.114 = (s32[]{:T(128)}, f32[2,2,512]{2,1,0:T(2,128)S(1)}, f32[2,2,512]{2,1,0:T(2,128)S(1)}, bf16[2,512,2,128]{3,1,2,0:T(8,128)(2,1)S(1)}, bf16[2048,2,128]...) while((s32[]{:T(128)}, f32[2,2,512]{2,1,0:T(2,128)S(1)}, ...), condition=%wide.region_17.18_spmd.clone, body=%wide.region_14.17_spmd.clone.sunk | while | flops 555745280 | bytes 18155616 | solution.py:65
  199.0 1.4 fusion.134
  200.4 2.1 exponential_reduce_fusion.11
  203.3 1.4 fusion.134
  204.7 2.1 exponential_reduce_fusion.11
  206.9 12.7 %pmax.30 = f32[2,1024]{1,0:T(2,128)S(1)} all-reduce(f32[2,1024]{1,0:T(2,128)S(1)} %bitcast.261), channel_id=1, replica_groups=mesh['pb'=16,'ka'=8] {'ka'}, use_global_device_ids=true, to_apply=%region_18.19 | all-reduce | flops 2048 | bytes 16384 | tf_op jit(solution)/shard_map/pmax | solution.py:13
  219.6 12.7 %psum.65 = f32[2,1024]{1,0:T(2,128)S(1)} all-reduce(f32[2,1024]{1,0:T(2,128)S(1)} %exponential_multiply_fusion.2), channel_id=1, replica_groups=mesh['pb'=16,'ka'=8] {'ka'}, use_global_device_ids=true, to_apply=%region_19.20 | all-reduce | flops 2048 | bytes 16384 | tf_op jit(solution)/shard_map/psum | solution.py:14
  232.3 6.3 while.112
  232.3 1.3 fusion.130
  233.6 1.8 exponential_reduce_fusion.9
  235.5 1.3 fusion.130
  236.8 1.8 exponential_reduce_fusion.9
  238.7 69.7 %pmax.31 = f32[2,2048]{1,0:T(2,128)S(1)} all-reduce(f32[2,2048]{1,0:T(2,128)S(1)} %reduce_max.55), channel_id=1, replica_groups=mesh['pb'=16,'ka'=8] {'pb'}, use_global_device_ids=true, to_apply=%region_25.26 | all-reduce | flops 4096 | bytes 32768 | tf_op jit(solution)/shard_map/pmax | solution.py:18
  308.5 69.5 %psum.66 = f32[2,2048]{1,0:T(2,128)S(1)} all-reduce(f32[2,2048]{1,0:T(2,128)S(1)} %exponential_multiply_fusion), channel_id=1, replica_groups=mesh['pb'=16,'ka'=8] {'pb'}, use_global_device_ids=true, to_apply=%region_27.28 | all-reduce | flops 4096 | bytes 32768 | tf_op jit(solution)/shard_map/psum | solution.py:19
  378.0 1.5 copy.24
  379.5 1.3 copy.38
  381.0 32.0 %while.118 = (s32[]{:T(128)}, f32[2,2048]{1,0:T(2,128)S(1)}, f32[2048,2,128]{0,2,1:T(8,128)}, f32[2,2,512]{2,1,0:T(2,128)S(1)}, bf16[2,512,2,128]{3,1,2,0:T(8,12...) while((s32[]{:T(128)}, f32[2,2048]{1,0:T(2,128)S(1)}, ...), condition=%wide.region_31.32_spmd.clone, body=%wide.region_28.31_spmd.clone.sunk | while | flops 1636832256 | bytes 61737192 | solution.py:107
  381.0 4.5 fusion.146
  386.3 7.2 fusion.148
  393.6 3.1 fusion.147
  396.7 4.5 fusion.146
  402.0 7.8 fusion.148
  409.8 3.1 fusion.147
  413.0 69.6 %psum.67 = f32[2,2048]{1,0:T(2,128)S(1)} all-reduce(f32[2,2048]{1,0:T(2,128)S(1)} %get-tuple-element.416), channel_id=1, replica_groups=mesh['pb'=16,'ka'=8] {'pb'}, use_global_device_ids=true, to_apply=%region_33.34 | all-reduce | flops 4096 | bytes 32768 | tf_op jit(solution)/shard_map/psum | solution.py:27
  482.6 7.1 while.115
  483.3 2.9 multiply_reduce_fusion.8
  486.9 2.9 multiply_reduce_fusion.8
  489.7 23.6 %all-reduce = (f32[2,1024]{1,0:T(2,128)S(1)}, f32[2,1024]{1,0:T(2,128)S(1)}) all-reduce(f32[2,1024]{1,0:T(2,128)S(1)} %bitcast.263, f32[2,1024]{1,0:T(2,128)S(1)} %bitcast.264), channel_id=1, replica_groups=mesh['pb'=16,'ka'=8] {'ka'}, use_global_device_ids=true, to_apply=%region_32.33 | all-reduce | flops 4096 | bytes 32768 | tf_op jit(solution)/shard_map/psum | solution.py:23
  513.4 6.9 while.116
  514.0 2.7 multiply_reduce_fusion.9
  517.5 2.7 multiply_reduce_fusion.9
  520.3 69.5 %psum.70 = f32[2,2048]{1,0:T(2,128)S(1)} all-reduce(f32[2,2048]{1,0:T(2,128)S(1)} %reduce_sum.110), channel_id=1, replica_groups=mesh['pb'=16,'ka'=8] {'pb'}, use_global_device_ids=true, to_apply=%region_42.43 | all-reduce | flops 4096 | bytes 32768 | tf_op jit(solution)/shard_map/psum | solution.py:27
  589.9 7.3 while.117
  590.6 2.9 multiply_reduce_fusion.10
  594.2 2.9 multiply_reduce_fusion.10
  597.1 12.9 %psum.71 = f32[2,2,512]{2,1,0:T(2,128)S(1)} all-reduce(f32[2,2,512]{2,1,0:T(2,128)S(1)} %get-tuple-element.420), channel_id=1, replica_groups=mesh['pb'=16,'ka'=8] {'ka'}, use_global_device_ids=true, to_apply=%region_46.47 | all-reduce | flops 2048 | bytes 16384 | tf_op jit(solution)/shard_map/psum | solution.py:23
  610.1 39.2 %while.119 = (s32[]{:T(128)}, f32[2048,2,128]{0,2,1:T(8,128)}, f32[2,512,2,128]{3,2,1,0:T(2,128)S(1)}, bf16[2,512,2,128]{3,1,2,0:T(8,128)(2,1)S(1)}, bf16[2048,2...) while((s32[]{:T(128)}, f32[2048,2,128]{0,2,1:T(8,128)}, ...), condition=%wide.region_48.49_spmd.clone, body=%wide.region_47.48_spmd.clone.sunk | while | flops 2197440512 | bytes 60313856 | solution.py:183
  610.1 1.3 fusion.157
  612.1 10.8 %subtract_convert_fusion.2 = bf16[2,512,2048]{2,1,0:T(8,128)(2,1)} fusion(f32[2,512,2048]{2,1,0:T(8,128)S(1)} %fusion.157, bf16[2048,2,128]{2,0,1:T(8,128)(2,1)S(1)} %copy-done.3, f32[2,512]{1,0:T(2,128)S(1)} %get-tuple-element.1377, f32[2,2048]{1,0:T(2,128)S(1)} %get-tuple-element.1378, f32[2,512]{1,0:T(2,128)S(1)} %get-tuple-element.1379, ...), kind=kOutput, calls=%fused_computation.94.clone.1 | convolution fusion | flops 585105408 | bytes 14010372 | tf_op jit(solution)/shard_map/while/body/eval_jaxpr/bhd,khd->hbk/dot_general | solution.py:151
  622.9 4.7 fusion.158
  627.6 1.3 fusion.159
  631.4 10.8 %subtract_convert_fusion.2 = bf16[2,512,2048]{2,1,0:T(8,128)(2,1)} fusion(f32[2,512,2048]{2,1,0:T(8,128)S(1)} %fusion.157, bf16[2048,2,128]{2,0,1:T(8,128)(2,1)S(1)} %copy-done.3, f32[2,512]{1,0:T(2,128)S(1)} %get-tuple-element.1377, f32[2,2048]{1,0:T(2,128)S(1)} %get-tuple-element.1378, f32[2,512]{1,0:T(2,128)S(1)} %get-tuple-element.1379, ...), kind=kOutput, calls=%fused_computation.94.clone.1 | convolution fusion | flops 585105408 | bytes 14010372 | tf_op jit(solution)/shard_map/while/body/eval_jaxpr/bhd,khd->hbk/dot_general | solution.py:151
  642.2 5.3 fusion.158
  647.5 1.3 fusion.159
  650.3 3.0 copy.44
  653.4 2.9 copy.45
  656.3 19.3 %reduce-scatter.4.cloned.1.call-done = f32[128,256]{1,0:T(8,128)} async-done(((f32[1024,256]{1,0:T(8,128)}), f32[128,256]{1,0:T(8,128)}) %reduce-scatter.4.cloned.1.call-update) | async-done | bytes 131088 | tf_op jit(solution)/shard_map/reduce_scatter | solution.py:196
  675.6 77.2 %reduce-scatter.6.cloned.1.call-done = f32[128,256]{1,0:T(8,128)} async-done(((f32[2048,256]{1,0:T(8,128)}), f32[128,256]{1,0:T(8,128)}) %reduce-scatter.6.cloned.1.call-update) | async-done | bytes 131088 | tf_op jit(solution)/shard_map/reduce_scatter | solution.py:199
  752.8 77.9 %reduce-scatter.8.cloned.1.call-done = f32[128,256]{1,0:T(8,128)} async-done(((f32[2048,256]{1,0:T(8,128)}), f32[128,256]{1,0:T(8,128)}) %reduce-scatter.8.cloned.1.call-update) | async-done | bytes 131088 | tf_op jit(solution)/shard_map/reduce_scatter | solution.py:200
  (131 shorter events, 15.9 us)
Async XLA Ops:
  7.2 668.4 %reduce-scatter.4.cloned.1.call-start = ((), (), s32[]{:S(2)}) async-start(), calls=%async_computation.3 | async-start | bytes 1179648 | tf_op jit(solution)/shard_map/reduce_scatter | solution.py:196
  52.7 76.0 %copy-start.4 = (f32[2,2,512]{2,1,0:T(2,128)}, f32[2,2,512]{2,1,0:T(2,128)S(1)}, u32[]{:S(2)}) copy-start(f32[2,2,512]{2,1,0:T(2,128)S(1)} %get-tuple-element.1681) | copy-start | bytes 24580
  232.3 148.5 %copy-start.6 = (bf16[1024,256]{1,0:T(8,128)(2,1)S(1)}, bf16[1024,256]{1,0:T(8,128)(2,1)}, u32[]{:S(2)}) copy-start(bf16[1024,256]{1,0:T(8,128)(2,1)} %param.26) | copy-start | bytes 1572868
  385.5 8.0 copy-start.2
  385.5 8.0 slice-start
  386.3 7.2 slice-start.1
  401.2 8.6 %copy-start.2 = (bf16[2048,2,128]{2,0,1:T(8,128)(2,1)S(1)}, bf16[2048,2,128]{2,0,1:T(8,128)(2,1)}, u32[]{:S(2)}) copy-start(bf16[2048,2,128]{2,0,1:T(8,128)(2,1)} %get-tuple-element.1507) | copy-start | bytes 3145732 | tf_op jit(solution)/shard_map/while
  401.2 8.6 %slice-start = ((s8[8388608]{0:T(1024)(128)(4,1)}), s8[4194304]{0:T(1024)(128)(4,1)S(1)}, s32[]{:S(2)}) async-start(s8[8388608]{0:T(1024)(128)(4,1)} %bitcast.248), calls=%async_computation.6 | async-start | bytes 8388608 | tf_op jit(solution)/shard_map/while
  402.0 7.8 slice-start.1
  513.3 76.5 %copy-start.5 = (f32[2,2,512]{2,1,0:T(2,128)S(1)}, f32[2,2,512]{2,1,0:T(2,128)}, u32[]{:S(2)}) copy-start(f32[2,2,512]{2,1,0:T(2,128)} %copy-done.4) | copy-start | bytes 24580
  589.8 20.2 %copy-start.1 = (f32[2,512,2,128]{3,2,1,0:T(2,128)S(1)}, f32[2,512,2,128]{3,2,1,0:T(2,128)}, u32[]{:S(2)}) copy-start(f32[2,512,2,128]{3,2,1,0:T(2,128)} %custom-call.3) | copy-start | bytes 3145732
  610.1 2.0 copy-start.3
  622.9 4.7 copy-start
  629.3 2.0 copy-start.3
  642.2 5.3 copy-start
  650.3 102.5 %reduce-scatter.6.cloned.1.call-start = ((), (), s32[]{:S(2)}) async-start(), calls=%async_computation.4 | async-start | bytes 2228224 | tf_op jit(solution)/shard_map/reduce_scatter | solution.py:199
  653.3 177.3 %reduce-scatter.8.cloned.1.call-start = ((), (), s32[]{:S(2)}) async-start(), calls=%async_computation.5 | async-start | bytes 2228224 | tf_op jit(solution)/shard_map/reduce_scatter | solution.py:200
Sparse Core Ops, SparseCore 0:
  650.4 25.1 reduce-scatter.3
  679.4 73.2 reduce-scatter.5
  756.9 73.6 reduce-scatter.7
where the time goes:
time: 838 us; the launch traced here: 837 us
  blocking collectives  513 us (61%)
  waiting for transfers between devices  174 us (21%)
  matrix products  94.6 us (11%)
  other arithmetic  25.4 us (3%)
  local copies, waits for them, and re-layouts  14.6 us (2%)
  between operations  14.1 us (2%)
    pmax x2, blocking collectives, col_merge(): highest = lax.pmax(peaks, 'pb')  146 us
    psum x2, blocking collectives, col_total(): return lax.psum(partial_sum, 'pb')  139 us
    psum x2, blocking collectives, col_merge(): return (highest, lax.psum(masses * jnp.exp(peaks - highest), 'pb'))  139 us
    reduce_scatter x1, waiting for transfers between devices, shards(): lax.psum_scatter(value_grad, 'pb', scatter_dimension=0, tiled=True)  77.9 us
    reduce_scatter x1, waiting for transfers between devices, shards(): lax.psum_scatter(key_grad, 'pb', scatter_dimension=0, tiled=True)  77.2 us
    dot_general x18, matrix products, scores(): jnp.einsum('bhd,khd->hbk', query_block, key_heads, preferred_element_type...  39.2 us
    psum x2, blocking collectives, row_total(): return lax.psum(partial_sum, 'ka')  36.5 us
    pmax x2, blocking collectives, row_merge(): highest = lax.pmax(peaks, 'ka')  27.6 us
  transfers between devices with their start and end apart: 3, of which 3 were waited for; matrix products, arithmetic and copies ran while one was open for 1% of the time, Pallas kernels for 0%

commit v1 on v0

v1 whole, which is shorter than its diff:
```python
import functools

import jax
import jax.numpy as jnp
from jax import lax
from jax.experimental import pallas as pl
from jax.experimental.pallas import tpu as pltpu
from jax.sharding import PartitionSpec as P

HD = 128
HEADS = 2
LANES = 128
RELAX = 0.9
LOG2E = 1.4426950408889634
MESH = pl.DeviceIdType.MESH
F32 = jnp.float32
BF16 = jnp.bfloat16
NEG = -1e30


def far(n):
    return min(n, 4 - n)


KA_OFFS = sorted(
    [(a, c) for a in range(4) for c in range(2) if a or c], key=lambda o: -far(o[0])
)
PB_OFFS = sorted(
    [(a, b) for a in range(4) for b in range(4) if a or b], key=lambda o: -far(o[0]) - far(o[1])
)
HOPS = (2, 1, 3)


def kernel(
    rows, cols, len_ref, q_hbm, k_hbm, v_hbm, o_hbm, gq_ref, gk_ref, gv_ref,
    q, k, v, o, qt, ot, kk, dd, bb, ra, rb, rw, ry, cv, cp,
    kab, pbb, dv, dk, dq, s1, p1, s2, sq,
    in_sem, ka_s, ka_r, pb_s, pb_r, s1_s, s1_r, s2_s, s2_r, sq_s, sq_r,
):
    tiles = cols // LANES
    blocks = rows // LANES
    groups = rows // 8
    pb, ka = lax.axis_index("pb"), lax.axis_index("ka")
    z, y = pb // 4, lax.rem(pb, 4)
    xx, cc = ka // 2, lax.rem(ka, 2)

    def ka_peer(off):
        return (pb, lax.rem(xx + off[0], 4) * 2 + lax.rem(cc + off[1], 2))

    def pb_peer(off):
        return (lax.rem(z + off[0], 4) * 4 + lax.rem(y + off[1], 4), ka)

    loads = [
        pltpu.make_async_copy(src, dst, in_sem.at[n])
        for n, (src, dst) in enumerate(((q_hbm, q), (k_hbm, k), (v_hbm, v), (o_hbm, o)))
    ]
    for copy in loads:
        copy.start()
    barrier = pltpu.get_barrier_semaphore()
    for off in KA_OFFS:
        pl.semaphore_signal(barrier, inc=1, device_id=ka_peer(off), device_id_type=MESH)
    for off in PB_OFFS:
        pl.semaphore_signal(barrier, inc=1, device_id=pb_peer(off), device_id_type=MESH)

    def ka_copies(r, h):
        return [
            pltpu.make_async_remote_copy(
                src_ref=kab.at[r, h, 0], dst_ref=kab.at[r, h, n + 1],
                send_sem=ka_s.at[r, h, n], recv_sem=ka_r.at[r, h, n],
                device_id=ka_peer(off), device_id_type=MESH,
            )
            for n, off in enumerate(KA_OFFS)
        ]

    def pb_copies(r, h):
        return [
            pltpu.make_async_remote_copy(
                src_ref=pbb.at[r, h, 0], dst_ref=pbb.at[r, h, n + 1],
                send_sem=pb_s.at[r, h, n], recv_sem=pb_r.at[r, h, n],
                device_id=pb_peer(off), device_id_type=MESH,
            )
            for n, off in enumerate(PB_OFFS)
        ]

    def start(copies):
        for copy in copies:
            copy.start()

    def arrive(copies):
        for copy in copies:
            copy.wait_recv()

    def drain(copies):
        for copy in copies:
            copy.wait_send()

    eye = lax.broadcasted_iota(jnp.int32, (LANES, LANES), 0) == lax.broadcasted_iota(
        jnp.int32, (LANES, LANES), 1
    )
    position = lax.broadcasted_iota(jnp.int32, (tiles, LANES), 0) * LANES + lax.broadcasted_iota(
        jnp.int32, (tiles, LANES), 1
    )
    valid = position < len_ref[0]

    def to_lanes(column):
        return jnp.sum(jnp.where(eye, column, 0.0), axis=0, keepdims=True)

    def spread_rows(compact, ref, h):
        for b in range(blocks):
            column = jnp.sum(jnp.where(eye, compact[b : b + 1, :], 0.0), axis=1, keepdims=True)
            ref[h, b * LANES : (b + 1) * LANES, :] = jnp.broadcast_to(column, (LANES, LANES))

    def spread_cols(compact, n, h):
        for t in range(tiles):
            cv[h, n, :, t * LANES : (t + 1) * LANES] = jnp.broadcast_to(
                compact[t : t + 1, :], (8, LANES)
            )

    def pack_cols(line, ref):
        for t in range(tiles):
            ref[t : t + 1, :] = line[:, t * LANES : (t + 1) * LANES]

    def wide(column):
        return jnp.concatenate([column] * tiles, axis=1)

    def fold(block, op):
        parts = [block[:, t * LANES : (t + 1) * LANES] for t in range(tiles)]
        while len(parts) > 1:
            parts = [op(a, b) for a, b in zip(parts[::2], parts[1::2])]
        return parts[0]

    def group(g):
        return pl.ds(pl.multiple_of(g * 8, 8), 8)

    def log2(x):
        return jnp.log(x) * LOG2E

    BIAS, RHO, PROB, BETA, GAMMA, SIGMA = range(6)
    LOGC, KAPPA = range(2)
    spread_cols(jnp.where(valid, 0.0, NEG), BIAS, 0)

    def head(h):
        return slice(h * HD, (h + 1) * HD)

    mm = 256

    def product(a, b, h, i):
        sl = pl.ds(pl.multiple_of(i * mm, mm), mm)
        return sl, lax.dot_general(
            a[sl, head(h)], b[:, head(h)], (((1,), (1,)), ((), ())), preferred_element_type=F32
        )

    def scores(h):
        def body(i, c):
            sl, s = product(q, k, h, i)
            kk[h, sl, :] = s * (HD**-0.5 * LOG2E) + cv[0, BIAS, 0:1, :]
            return c

        lax.fori_loop(0, rows // mm, body, 0)

        def sweep(g, c):
            sl = group(g)
            s = kk[h, sl, :]
            peak = fold(s, jnp.maximum)
            ra[h, sl, :] = peak
            rb[h, sl, :] = fold(jnp.exp2(s - wide(peak)), jnp.add)
            return c

        lax.fori_loop(0, groups, sweep, 0, unroll=4)
        for b in range(blocks):
            sl = slice(b * LANES, (b + 1) * LANES)
            peak = ra[h, sl, :]
            highest = jnp.max(peak, axis=1, keepdims=True)
            mass = jnp.sum(rb[h, sl, :] * jnp.exp2(peak - highest), axis=1, keepdims=True)
            kab[0, h, 0, 0, b : b + 1, :] = to_lanes(highest)
            kab[0, h, 0, 1, b : b + 1, :] = to_lanes(mass)

    loads[0].wait()
    loads[1].wait()
    scores(0)
    pl.semaphore_wait(barrier, len(KA_OFFS) + len(PB_OFFS))
    start(ka_copies(0, 0))
    scores(1)
    start(ka_copies(0, 1))

    loads[2].wait()
    loads[3].wait()
    for h in range(HEADS):

        def body(i, c):
            sl, s = product(o, v, h, i)
            dd[h, sl, :] = s
            return c

        lax.fori_loop(0, rows // mm, body, 0)
    for h in range(HEADS):
        qt[h] = q[:, head(h)].astype(F32).T.astype(BF16)
        ot[h] = o[:, head(h)].astype(F32).T.astype(BF16)

    def merge(parts):
        highest = parts[0][0]
        for m, _ in parts[1:]:
            highest = jnp.maximum(highest, m)
        mass = sum(s * jnp.exp2(m - highest) for m, s in parts)
        return highest + log2(mass)

    def first_columns(h):
        pot = -merge([(kab[0, h, n, 0], kab[0, h, n, 1]) for n in range(8)])
        spread_rows(pot, rw, h)

        def peaks(g, acc):
            sl = group(g)
            return jnp.maximum(acc, kk[h, sl, :] + wide(rw[h, sl, :]))

        acc = lax.fori_loop(0, groups, peaks, jnp.full((8, cols), NEG, F32), unroll=4)
        peak = jnp.maximum(jnp.max(acc, axis=0, keepdims=True), -1e4)
        lift = jnp.broadcast_to(peak, (8, cols))

        def masses(g, acc):
            sl = group(g)
            e = jnp.exp2(kk[h, sl, :] + wide(rw[h, sl, :]) - lift)
            kk[h, sl, :] = e
            return acc + e

        acc = lax.fori_loop(0, groups, masses, jnp.zeros((8, cols), F32), unroll=4)
        pack_cols(peak, pbb.at[0, h, 0, 0])
        pack_cols(jnp.sum(acc, axis=0, keepdims=True), pbb.at[0, h, 0, 1])

    for h in range(HEADS):
        arrive(ka_copies(0, h))
        first_columns(h)
        start(pb_copies(0, h))

    def row_sums(n, r, h):
        x = cv[h, n]

        def body(g, c):
            sl = group(g)
            ra[h, sl, :] = fold(kk[h, sl, :] * x, jnp.add)
            return c

        lax.fori_loop(0, groups, body, 0, unroll=4)
        pack_rows(r, h)

    def pack_rows(r, h):
        for b in range(blocks):
            column = jnp.sum(ra[h, b * LANES : (b + 1) * LANES, :], axis=1, keepdims=True)
            kab[r, h, 0, 0, b : b + 1, :] = to_lanes(column)

    def row_total(r, h):
        return sum(kab[r, h, n, 0] for n in range(8))

    def col_total(r, h, n):
        return sum(pbb[r, h, m, n] for m in range(16))

    for h in range(HEADS):
        arrive(pb_copies(0, h))
        logc = merge([(pbb[0, h, n, 0], pbb[0, h, n, 1]) for n in range(16)])
        logc = jnp.where(valid, logc, 0.0)
        kappa = jnp.where(valid, jnp.exp2(pbb[0, h, 0, 0] - logc), 0.0)
        cp[h, LOGC] = logc
        cp[h, KAPPA] = kappa
        spread_cols(kappa * jnp.exp2((1.0 - RELAX) * logc), RHO, h)
        spread_cols(kappa * jnp.exp2(logc), SIGMA, h)
        row_sums(RHO, 1, h)
        start(ka_copies(1, h))

    def second_columns(h):
        spread_rows(1.0 / row_total(1, h), rw, h)

        def body(g, accs):
            sl = group(g)
            kw = kk[h, sl, :] * wide(rw[h, sl, :])
            return accs[0] + kw, accs[1] + kw * dd[h, sl, :]

        zero = jnp.zeros((8, cols), F32)
        mass, adjoint = lax.fori_loop(0, groups, body, (zero, zero), unroll=2)
        kappa = cp[h, KAPPA]
        pack_cols(jnp.sum(mass, axis=0, keepdims=True), pbb.at[1, h, 0, 0])
        pack_cols(jnp.sum(adjoint, axis=0, keepdims=True), pbb.at[1, h, 0, 1])
        pbb[1, h, 0, 0] = pbb[1, h, 0, 0] * kappa
        pbb[1, h, 0, 1] = pbb[1, h, 0, 1] * kappa

    for h in range(HEADS):
        arrive(ka_copies(1, h))
        second_columns(h)
        start(pb_copies(1, h))

    def second_rows(h):
        mass = jnp.where(valid, col_total(1, h, 0), 1.0)
        kappa = cp[h, KAPPA]
        power = jnp.exp2((1.0 - RELAX) * cp[h, LOGC] - RELAX * log2(mass))
        spread_cols(kappa * power, PROB, h)
        spread_cols(RELAX * power * col_total(1, h, 1) * kappa / mass, BETA, h)

        def body(g, c):
            sl = group(g)
            t = (kk[h, sl, :] * wide(rw[h, sl, :])) * (dd[h, sl, :] * cv[h, PROB] - cv[h, BETA])
            dd[h, sl, :] = t
            ra[h, sl, :] = fold(t, jnp.add)
            return c

        lax.fori_loop(0, groups, body, 0, unroll=2)
        pack_rows(2, h)

    for h in range(HEADS):
        arrive(pb_copies(1, h))
        second_rows(h)
        start(ka_copies(2, h))

    def rs_first(w, h, part):
        copies = []
        for a in HOPS:
            ty, tz = lax.rem(y + a, 4), lax.rem(z + a, 4)
            if h == 0:
                src, dev = part.at[h, :, ty], (z * 4 + ty, ka)
            else:
                src, dev = part.at[h, tz], (tz * 4 + y, ka)
            copies.append(
                pltpu.make_async_remote_copy(
                    src_ref=src, dst_ref=s1.at[w, h, a - 1],
                    send_sem=s1_s.at[w, h, a - 1], recv_sem=s1_r.at[w, h, a - 1],
                    device_id=dev, device_id_type=MESH,
                )
            )
        return copies

    def rs_second(w, h):
        copies = []
        for a in HOPS:
            ty, tz = lax.rem(y + a, 4), lax.rem(z + a, 4)
            t, dev = (tz, (tz * 4 + y, ka)) if h == 0 else (ty, (z * 4 + ty, ka))
            copies.append(
                pltpu.make_async_remote_copy(
                    src_ref=p1.at[w, h, t], dst_ref=s2.at[w, h, a - 1],
                    send_sem=s2_s.at[w, h, a - 1], recv_sem=s2_r.at[w, h, a - 1],
                    device_id=dev, device_id_type=MESH,
                )
            )
        return copies

    def rs_middle(w, h, part):
        arrive(rs_first(w, h, part))
        copies = rs_second(w, h)
        for n, a in enumerate(HOPS + (0,)):
            t = lax.rem((z if h == 0 else y) + a, 4)

            def body(i, c):
                sl = pl.ds(pl.multiple_of(i * 32, 32), 32)
                own = part[h, t, y, sl] if h == 0 else part[h, z, t, sl]
                p1[w, h, t, sl] = own + s1[w, h, 0, t, sl] + s1[w, h, 1, t, sl] + s1[w, h, 2, t, sl]
                return c

            lax.fori_loop(0, 4, body, 0)
            if a:
                copies[n].start()

    def rs_last(w, h, scale, out):
        arrive(rs_second(w, h))
        t = z if h == 0 else y
        total = (p1[w, h, t] + s2[w, h, 0]) + (s2[w, h, 1] + s2[w, h, 2])
        out[:, head(h)] = total.T * scale

    def by_columns(lhs, part, h):
        def body(n, c):
            sl = pl.ds(pl.multiple_of(n * 256, 256), 256)
            res = jnp.dot(lhs[h], bb[:, sl], preferred_element_type=F32)
            part[h, n // 2, 2 * lax.rem(n, 2)] = res[:, :LANES]
            part[h, n // 2, 2 * lax.rem(n, 2) + 1] = res[:, LANES:]
            return c

        lax.fori_loop(0, cols // 256, body, 0)

    def value_part(h):
        def body(g, c):
            sl = pl.ds(pl.multiple_of(g * 16, 16), 16)
            w = rw[h, sl, :]
            prob = (kk[h, sl, :] * wide(w)) * cv[h, PROB, 0:1, :]
            bb[sl, :] = prob.astype(BF16)
            return c

        lax.fori_loop(0, rows // 16, body, 0, unroll=2)
        by_columns(ot, dv, h)

    for h in range(HEADS):
        value_part(h)

    def first_adjoint(h):
        total = row_total(2, h)
        spread_rows(total, ry, h)

        def body(g, acc):
            sl = group(g)
            yw = ry[h, sl, :] * rw[h, sl, :]
            ry[h, sl, :] = yw
            return acc + kk[h, sl, :] * wide(yw)

        acc = lax.fori_loop(0, groups, body, jnp.zeros((8, cols), F32), unroll=4)
        pack_cols(jnp.sum(acc, axis=0, keepdims=True), pbb.at[2, h, 0, 0])
        pbb[2, h, 0, 0] = pbb[2, h, 0, 0] * cp[h, KAPPA]

    for h in range(HEADS):
        arrive(ka_copies(2, h))
        first_adjoint(h)
        start(pb_copies(2, h))
    for h in range(HEADS):
        start(rs_first(0, h, dv))

    for h in range(HEADS):
        arrive(pb_copies(2, h))
        adj = -jnp.exp2((1.0 - RELAX) * cp[h, LOGC]) * col_total(2, h, 0)
        spread_cols(RELAX * cp[h, KAPPA] * adj, GAMMA, h)
        row_sums(GAMMA, 3, h)
        start(ka_copies(3, h))

    for h in range(HEADS):

        def body(g, c):
            sl = group(g)
            yw = wide(ry[h, sl, :])
            dd[h, sl, :] = dd[h, sl, :] - kk[h, sl, :] * (yw * cv[h, RHO] + cv[h, GAMMA])
            return c

        lax.fori_loop(0, groups, body, 0, unroll=2)

    def sq_copies(h):
        copies = []
        for n, off in enumerate(KA_OFFS):
            dev = ka_peer(off)
            copies.append(
                pltpu.make_async_remote_copy(
                    src_ref=dq.at[h, dev[1]], dst_ref=sq.at[h, n],
                    send_sem=sq_s.at[h, n], recv_sem=sq_r.at[h, n],
                    device_id=dev, device_id_type=MESH,
                )
            )
        return copies

    for h in range(HEADS):
        arrive(ka_copies(3, h))
        spread_rows(-row_total(3, h), ry, h)

        def body(g, c):
            sl = pl.ds(pl.multiple_of(g * 16, 16), 16)
            zw = wide(ry[h, sl, :])
            bb[sl, :] = (dd[h, sl, :] - kk[h, sl, :] * (zw * cv[h, SIGMA, 0:1, :])).astype(BF16)
            return c

        lax.fori_loop(0, rows // 16, body, 0, unroll=2)
        by_columns(qt, dk, h)
        start(rs_first(1, h, dk))

        def body(i, c):
            sl = pl.ds(pl.multiple_of(i * mm, mm), mm)
            res = jnp.dot(bb[sl, :], k[:, head(h)], preferred_element_type=F32)
            for n in range(mm // LANES):
                dq[h, i * (mm // LANES) + n] = res[n * LANES : (n + 1) * LANES]
            return c

        lax.fori_loop(0, rows // mm, body, 0)
        start(sq_copies(h))

    for w, part in ((0, dv), (1, dk)):
        for h in range(HEADS):
            rs_middle(w, h, part)
    for h in range(HEADS):
        rs_last(0, h, 1.0, gv_ref)
    for h in range(HEADS):
        arrive(sq_copies(h))
        total = dq[h, ka]
        for n in range(7):
            total = total + sq[h, n]
        gq_ref[:, head(h)] = total * HD**-0.5
    for h in range(HEADS):
        rs_last(1, h, HD**-0.5, gk_ref)

    for h in range(HEADS):
        for r in range(4):
            drain(ka_copies(r, h))
        for r in range(3):
            drain(pb_copies(r, h))
        for w, part in ((0, dv), (1, dk)):
            drain(rs_first(w, h, part))
            drain(rs_second(w, h))
        drain(sq_copies(h))


def shards(queries, keys, values, grad_out, key_lengths):
    rows, width = queries.shape
    cols = keys.shape[0]
    vmem = lambda *shape: pltpu.VMEM(shape, F32)
    half = lambda *shape: pltpu.VMEM(shape, BF16)
    dma = lambda *shape: pltpu.SemaphoreType.DMA(shape)
    scratch = [
        half(rows, width), half(cols, width), half(cols, width), half(rows, width),
        half(HEADS, HD, rows), half(HEADS, HD, rows),
        vmem(HEADS, rows, cols), vmem(HEADS, rows, cols), half(rows, cols),
        vmem(HEADS, rows, LANES), vmem(HEADS, rows, LANES),
        vmem(HEADS, rows, LANES), vmem(HEADS, rows, LANES),
        vmem(HEADS, 6, 8, cols), vmem(HEADS, 2, cols // LANES, LANES),
        vmem(4, HEADS, 8, 2, rows // LANES, LANES),
        vmem(3, HEADS, 16, 2, cols // LANES, LANES),
        vmem(HEADS, 4, 4, HD, LANES), vmem(HEADS, 4, 4, HD, LANES),
        vmem(HEADS, rows // LANES, LANES, HD),
        vmem(2, HEADS, 3, 4, HD, LANES), vmem(2, HEADS, 4, HD, LANES),
        vmem(2, HEADS, 3, HD, LANES), vmem(HEADS, 7, LANES, HD),
        dma(4), dma(4, HEADS, 7), dma(4, HEADS, 7), dma(3, HEADS, 15), dma(3, HEADS, 15),
        dma(2, HEADS, 3), dma(2, HEADS, 3), dma(2, HEADS, 3), dma(2, HEADS, 3),
        dma(HEADS, 7), dma(HEADS, 7),
    ]
    hbm = pl.BlockSpec(memory_space=pl.ANY)
    here = pl.BlockSpec(memory_space=pltpu.VMEM)
    return pl.pallas_call(
        functools.partial(kernel, rows, cols),
        out_shape=(
            jax.ShapeDtypeStruct((rows // 8, width), F32),
            jax.ShapeDtypeStruct((cols // 16, width), F32),
            jax.ShapeDtypeStruct((cols // 16, width), F32),
        ),
        in_specs=[pl.BlockSpec(memory_space=pltpu.SMEM), hbm, hbm, hbm, hbm],
        out_specs=(here, here, here),
        scratch_shapes=scratch,
        compiler_params=pltpu.CompilerParams(
            collective_id=0, has_side_effects=True, vmem_limit_bytes=60 * 2**20
        ),
        cost_estimate=pl.CostEstimate(
            flops=24 * rows * cols * HD, bytes_accessed=2**22, transcendentals=4 * rows * cols
        ),
    )(key_lengths, queries, keys, values, grad_out)


def solution(mesh):
    placed = (P("pb", None), P("ka", None), P("ka", None), P("pb", None), P("ka"))
    return jax.shard_map(
        shards,
        mesh=mesh,
        in_specs=placed,
        out_specs=(P(("pb", "ka"), None), P(("ka", "pb"), None), P(("ka", "pb"), None)),
        check_vma=False,
    )
```

time: 838 us -> 103 us (0.12)
  blocking collectives: 513 us -> 0 us
  waiting for transfers between devices: 174 us -> 0 us
  Pallas kernels: 0 us -> 98.8 us
  matrix products: 94.6 us -> 0 us
  other arithmetic: 25.4 us -> 0 us
  between operations: 14.1 us -> 1.3 us
  local copies, waits for them, and re-layouts: 14.6 us -> 3.21 us
    psum x8 -> x0, blocking collectives: 340 us -> none  [the longest x2 139 us: col_total(): return lax.psum(partial_sum, 'pb')]
    reduce_scatter x3 -> x0, waiting for transfers between devices: 174 us -> none  [the longest x1 77.9 us: shards(): lax.psum_scatter(value_grad, 'pb', scatter_dimension=0, tiled=True)]
    pmax x4 -> x0, blocking collectives: 173 us -> none  [the longest x2 146 us: col_merge(): highest = lax.pmax(peaks, 'pb')]
    pallas_call x0 -> x1, Pallas kernels: none -> 98.8 us  [shards(): pl.pallas_call(functools.partial(kernel, rows, cols), out_shape=(jax.Shap...]
    dot_general x28 -> x0, matrix products: 94.6 us -> none  [the longest x18 39.2 us: scores(): jnp.einsum('bhd,khd->hbk', query_block, key_heads, preferred_element_type...]
    reduce_sum x11 -> x0, other arithmetic: 15.5 us -> none  [the longest x4 8.07 us: row_one_block(): return (peak, jnp.sum(jnp.exp(logits - peak[..., None]), axis=-1))]
    lt x14 -> x0, other arithmetic: 9.52 us -> none  [shards(): is_valid = jnp.arange(col_count, dtype=jnp.int32) < key_lengths[0]]
  transfers between devices with their start and end apart: 3 -> 0, of which waited for: 3 -> 0; matrix products, arithmetic and copies ran while one was open for 1% -> 0% of each run, Pallas kernels for 0% -> 0%
where the time goes in v1:
time: 103 us
  Pallas kernels  98.8 us (96%)
  local copies, waits for them, and re-layouts  3.21 us (3%)
  between operations  1.3 us (1%)
    pallas_call x1, Pallas kernels, shards(): pl.pallas_call(functools.partial(kernel, rows, cols), out_shape=(jax.Shap...  98.8 us
    unnamed x7, local copies, waits for them, and re-layouts  3.21 us

profile of v1, /device:TPU:0, one launch (start us, length us, event | category | flops | bytes accessed | tf_op | source)
XLA Modules:
  0.0 103.3 jit_solution(15450881197627682289)
XLA Ops:
  1.3 98.8 %shard_map.76 = (f32[128,256]{1,0:T(8,128)}, f32[128,256]{1,0:T(8,128)}, f32[128,256]{1,0:T(8,128)}) custom-call(s32[1]{0:T(128)S(6)} %copy.11.len_ref, bf16[1024,256]{1,0:T(8,128)(2,1)} %q_hbm.1, bf16[2048,256]{1,0:T(8,128)(2,1)} %k_hbm.1, bf16[2048,256]{1,0:T(8,128)(2,1)} %v_hbm.1, bf16[1024,256]{1,0:T(8,128)(2,1)} %o_hbm.1), custom_call_target="tpu_custom_call" | custom-call | flops 6442450944 | bytes 4194304 | tf_op jit(solution)/shard_map/pallas_call | solution.py:513
  100.0 0.0 copy-start.1
  100.1 1.6 %copy.12 = f32[128,256]{1,0:T(8,128)} copy(f32[128,256]{1,0:T(8,128)} %get-tuple-element.6) | data formatting | bytes 262144
  101.7 0.0 copy-done.1
  101.7 0.0 copy-start
  101.7 0.7 copy.13
  102.3 0.3 copy-done
  102.6 0.7 copy.14
Async XLA Ops:
  100.0 1.6 %copy-start.1 = (f32[128,256]{1,0:T(8,128)S(1)}, f32[128,256]{1,0:T(8,128)}, u32[]{:S(2)}) copy-start(f32[128,256]{1,0:T(8,128)} %get-tuple-element.7) | copy-start | bytes 393220
  101.7 1.0 copy-start

commit v2 on v1

--- a/solution.py
+++ b/solution.py
@@ -142,21 +142,13 @@
     def head(h):
         return slice(h * HD, (h + 1) * HD)
 
-    mm = 256
-
-    def product(a, b, h, i):
-        sl = pl.ds(pl.multiple_of(i * mm, mm), mm)
-        return sl, lax.dot_general(
-            a[sl, head(h)], b[:, head(h)], (((1,), (1,)), ((), ())), preferred_element_type=F32
+    def product(a, b, h):
+        return lax.dot_general(
+            a[:, head(h)], b[:, head(h)], (((1,), (1,)), ((), ())), preferred_element_type=F32
         )
 
     def scores(h):
-        def body(i, c):
-            sl, s = product(q, k, h, i)
-            kk[h, sl, :] = s * (HD**-0.5 * LOG2E) + cv[0, BIAS, 0:1, :]
-            return c
-
-        lax.fori_loop(0, rows // mm, body, 0)
+        kk[h] = product(q, k, h) * (HD**-0.5 * LOG2E) + cv[0, BIAS, 0:1, :]
 
         def sweep(g, c):
             sl = group(g)
@@ -166,7 +158,7 @@
             rb[h, sl, :] = fold(jnp.exp2(s - wide(peak)), jnp.add)
             return c
 
-        lax.fori_loop(0, groups, sweep, 0, unroll=4)
+        lax.fori_loop(0, groups, sweep, 0, unroll=16)
         for b in range(blocks):
             sl = slice(b * LANES, (b + 1) * LANES)
             peak = ra[h, sl, :]
@@ -183,19 +175,8 @@
     scores(1)
     start(ka_copies(0, 1))
 
-    loads[2].wait()
-    loads[3].wait()
-    for h in range(HEADS):
-
-        def body(i, c):
-            sl, s = product(o, v, h, i)
-            dd[h, sl, :] = s
-            return c
-
-        lax.fori_loop(0, rows // mm, body, 0)
-    for h in range(HEADS):
-        qt[h] = q[:, head(h)].astype(F32).T.astype(BF16)
-        ot[h] = o[:, head(h)].astype(F32).T.astype(BF16)
+    def output_product(h):
+        dd[h] = product(o, v, h)
 
     def merge(parts):
         highest = parts[0][0]
@@ -212,17 +193,22 @@
             sl = group(g)
             return jnp.maximum(acc, kk[h, sl, :] + wide(rw[h, sl, :]))
 
-        acc = lax.fori_loop(0, groups, peaks, jnp.full((8, cols), NEG, F32), unroll=4)
+        acc = lax.fori_loop(0, groups, peaks, jnp.full((8, cols), NEG, F32), unroll=8)
         peak = jnp.maximum(jnp.max(acc, axis=0, keepdims=True), -1e4)
-        lift = jnp.broadcast_to(peak, (8, cols))
+        cv[h, PROB] = jnp.broadcast_to(peak, (8, cols))
 
         def masses(g, acc):
-            sl = group(g)
-            e = jnp.exp2(kk[h, sl, :] + wide(rw[h, sl, :]) - lift)
-            kk[h, sl, :] = e
-            return acc + e
-
-        acc = lax.fori_loop(0, groups, masses, jnp.zeros((8, cols), F32), unroll=4)
+            sl = pl.ds(pl.multiple_of(g * 32, 32), 32)
+            pot = rw[h, sl, :]
+            out = []
+            for t in range(tiles):
+                cs = slice(t * LANES, (t + 1) * LANES)
+                e = jnp.exp2(kk[h, sl, cs] + pot - cv[h, PROB, 0:1, cs])
+                kk[h, sl, cs] = e
+                out.append(acc[:, cs] + ((e[:8] + e[8:16]) + (e[16:24] + e[24:])))
+            return jnp.concatenate(out, axis=1)
+
+        acc = lax.fori_loop(0, rows // 32, masses, jnp.zeros((8, cols), F32))
         pack_cols(peak, pbb.at[0, h, 0, 0])
         pack_cols(jnp.sum(acc, axis=0, keepdims=True), pbb.at[0, h, 0, 1])
 
@@ -239,7 +225,7 @@
             ra[h, sl, :] = fold(kk[h, sl, :] * x, jnp.add)
             return c
 
-        lax.fori_loop(0, groups, body, 0, unroll=4)
+        lax.fori_loop(0, groups, body, 0, unroll=8)
         pack_rows(r, h)
 
     def pack_rows(r, h):
@@ -253,7 +239,10 @@
     def col_total(r, h, n):
         return sum(pbb[r, h, m, n] for m in range(16))
 
-    for h in range(HEADS):
+    loads[2].wait()
+    loads[3].wait()
+    for h in range(HEADS):
+        output_product(h)
         arrive(pb_copies(0, h))
         logc = merge([(pbb[0, h, n, 0], pbb[0, h, n, 1]) for n in range(16)])
         logc = jnp.where(valid, logc, 0.0)
@@ -274,7 +263,7 @@
             return accs[0] + kw, accs[1] + kw * dd[h, sl, :]
 
         zero = jnp.zeros((8, cols), F32)
-        mass, adjoint = lax.fori_loop(0, groups, body, (zero, zero), unroll=2)
+        mass, adjoint = lax.fori_loop(0, groups, body, (zero, zero), unroll=4)
         kappa = cp[h, KAPPA]
         pack_cols(jnp.sum(mass, axis=0, keepdims=True), pbb.at[1, h, 0, 0])
         pack_cols(jnp.sum(adjoint, axis=0, keepdims=True), pbb.at[1, h, 0, 1])
@@ -285,6 +274,8 @@
         arrive(ka_copies(1, h))
         second_columns(h)
         start(pb_copies(1, h))
+        qt[h] = q[:, head(h)].astype(F32).T.astype(BF16)
+        ot[h] = o[:, head(h)].astype(F32).T.astype(BF16)
 
     def second_rows(h):
         mass = jnp.where(valid, col_total(1, h, 0), 1.0)
@@ -300,7 +291,7 @@
             ra[h, sl, :] = fold(t, jnp.add)
             return c
 
-        lax.fori_loop(0, groups, body, 0, unroll=2)
+        lax.fori_loop(0, groups, body, 0, unroll=4)
         pack_rows(2, h)
 
     for h in range(HEADS):
@@ -308,86 +299,91 @@
         second_rows(h)
         start(ka_copies(2, h))
 
-    def rs_first(w, h, part):
+    HH = HD // 2
+
+    def half(e):
+        return slice(e * HH, (e + 1) * HH)
+
+    def along(e, t):
+        return ((z * 4 + t), ka) if e == 0 else ((t * 4 + y), ka)
+
+    def rs_first(w, h, e, part):
         copies = []
         for a in HOPS:
-            ty, tz = lax.rem(y + a, 4), lax.rem(z + a, 4)
-            if h == 0:
-                src, dev = part.at[h, :, ty], (z * 4 + ty, ka)
-            else:
-                src, dev = part.at[h, tz], (tz * 4 + y, ka)
+            t = lax.rem((y if e == 0 else z) + a, 4)
             copies.append(
                 pltpu.make_async_remote_copy(
-                    src_ref=src, dst_ref=s1.at[w, h, a - 1],
-                    send_sem=s1_s.at[w, h, a - 1], recv_sem=s1_r.at[w, h, a - 1],
-                    device_id=dev, device_id_type=MESH,
+                    src_ref=part.at[h, :, t, half(e)] if e == 0 else part.at[h, t, :, half(e)],
+                    dst_ref=s1.at[w, h, e, a - 1],
+                    send_sem=s1_s.at[w, h, e, a - 1], recv_sem=s1_r.at[w, h, e, a - 1],
+                    device_id=along(e, t), device_id_type=MESH,
                 )
             )
         return copies
 
-    def rs_second(w, h):
+    def rs_second(w, h, e):
         copies = []
         for a in HOPS:
-            ty, tz = lax.rem(y + a, 4), lax.rem(z + a, 4)
-            t, dev = (tz, (tz * 4 + y, ka)) if h == 0 else (ty, (z * 4 + ty, ka))
+            t = lax.rem((z if e == 0 else y) + a, 4)
             copies.append(
                 pltpu.make_async_remote_copy(
-                    src_ref=p1.at[w, h, t], dst_ref=s2.at[w, h, a - 1],
-                    send_sem=s2_s.at[w, h, a - 1], recv_sem=s2_r.at[w, h, a - 1],
-                    device_id=dev, device_id_type=MESH,
+                    src_ref=p1.at[w, h, e, t], dst_ref=s2.at[w, h, e, a - 1],
+                    send_sem=s2_s.at[w, h, e, a - 1], recv_sem=s2_r.at[w, h, e, a - 1],
+                    device_id=along(1 - e, t), device_id_type=MESH,
                 )
             )
         return copies
 
+    def rs_start(w, h, part):
+        for e in range(2):
+            start(rs_first(w, h, e, part))
+
     def rs_middle(w, h, part):
-        arrive(rs_first(w, h, part))
-        copies = rs_second(w, h)
-        for n, a in enumerate(HOPS + (0,)):
-            t = lax.rem((z if h == 0 else y) + a, 4)
-
-            def body(i, c):
-                sl = pl.ds(pl.multiple_of(i * 32, 32), 32)
-                own = part[h, t, y, sl] if h == 0 else part[h, z, t, sl]
-                p1[w, h, t, sl] = own + s1[w, h, 0, t, sl] + s1[w, h, 1, t, sl] + s1[w, h, 2, t, sl]
-                return c
-
-            lax.fori_loop(0, 4, body, 0)
-            if a:
-                copies[n].start()
+        for e in range(2):
+            arrive(rs_first(w, h, e, part))
+            for t in range(4):
+                own = part[h, t, y, half(e)] if e == 0 else part[h, z, t, half(e)]
+                p1[w, h, e, t] = (own + s1[w, h, e, 0, t]) + (s1[w, h, e, 1, t] + s1[w, h, e, 2, t])
+            start(rs_second(w, h, e))
 
     def rs_last(w, h, scale, out):
-        arrive(rs_second(w, h))
-        t = z if h == 0 else y
-        total = (p1[w, h, t] + s2[w, h, 0]) + (s2[w, h, 1] + s2[w, h, 2])
-        out[:, head(h)] = total.T * scale
+        halves = []
+        for e in range(2):
+            arrive(rs_second(w, h, e))
+            t = z if e == 0 else y
+            halves.append((p1[w, h, e, t] + s2[w, h, e, 0]) + (s2[w, h, e, 1] + s2[w, h, e, 2]))
+        out[:, head(h)] = jnp.concatenate(halves, axis=0).T * scale
+
+    STRIP = 512
+
+    def strips(body):
+        for n in range(cols // STRIP):
+            cs = slice(n * STRIP, (n + 1) * STRIP)
+            lax.fori_loop(0, rows // 16, functools.partial(body, cs), 0, unroll=4)
+
+    def strip_wide(column):
+        return jnp.concatenate([column] * (STRIP // LANES), axis=1)
+
+    def rows16(g):
+        return pl.ds(pl.multiple_of(g * 16, 16), 16)
 
     def by_columns(lhs, part, h):
-        def body(n, c):
-            sl = pl.ds(pl.multiple_of(n * 256, 256), 256)
-            res = jnp.dot(lhs[h], bb[:, sl], preferred_element_type=F32)
-            part[h, n // 2, 2 * lax.rem(n, 2)] = res[:, :LANES]
-            part[h, n // 2, 2 * lax.rem(n, 2) + 1] = res[:, LANES:]
+        res = jnp.dot(lhs[h], bb[...], preferred_element_type=F32)
+        for t in range(tiles):
+            part[h, t // 4, t % 4] = res[:, t * LANES : (t + 1) * LANES]
+
+    def value_part(h):
+        def body(cs, g, c):
+            sl = rows16(g)
+            prob = (kk[h, sl, cs] * strip_wide(rw[h, sl, :])) * cv[h, PROB, 0:1, cs]
+            bb[sl, cs] = prob.astype(BF16)
             return c
 
-        lax.fori_loop(0, cols // 256, body, 0)
-
-    def value_part(h):
-        def body(g, c):
-            sl = pl.ds(pl.multiple_of(g * 16, 16), 16)
-            w = rw[h, sl, :]
-            prob = (kk[h, sl, :] * wide(w)) * cv[h, PROB, 0:1, :]
-            bb[sl, :] = prob.astype(BF16)
-            return c
-
-        lax.fori_loop(0, rows // 16, body, 0, unroll=2)
+        strips(body)
         by_columns(ot, dv, h)
 
-    for h in range(HEADS):
-        value_part(h)
-
     def first_adjoint(h):
-        total = row_total(2, h)
-        spread_rows(total, ry, h)
+        spread_rows(row_total(2, h), ry, h)
 
         def body(g, acc):
             sl = group(g)
@@ -395,7 +391,7 @@
             ry[h, sl, :] = yw
             return acc + kk[h, sl, :] * wide(yw)
 
-        acc = lax.fori_loop(0, groups, body, jnp.zeros((8, cols), F32), unroll=4)
+        acc = lax.fori_loop(0, groups, body, jnp.zeros((8, cols), F32), unroll=8)
         pack_cols(jnp.sum(acc, axis=0, keepdims=True), pbb.at[2, h, 0, 0])
         pbb[2, h, 0, 0] = pbb[2, h, 0, 0] * cp[h, KAPPA]
 
@@ -403,8 +399,11 @@
         arrive(ka_copies(2, h))
         first_adjoint(h)
         start(pb_copies(2, h))
-    for h in range(HEADS):
-        start(rs_first(0, h, dv))
+        if h == 0:
+            value_part(0)
+    rs_start(0, 0, dv)
+    value_part(1)
+    rs_start(0, 1, dv)
 
     for h in range(HEADS):
         arrive(pb_copies(2, h))
@@ -412,16 +411,6 @@
         spread_cols(RELAX * cp[h, KAPPA] * adj, GAMMA, h)
         row_sums(GAMMA, 3, h)
         start(ka_copies(3, h))
-
-    for h in range(HEADS):
-
-        def body(g, c):
-            sl = group(g)
-            yw = wide(ry[h, sl, :])
-            dd[h, sl, :] = dd[h, sl, :] - kk[h, sl, :] * (yw * cv[h, RHO] + cv[h, GAMMA])
-            return c
-
-        lax.fori_loop(0, groups, body, 0, unroll=2)
 
     def sq_copies(h):
         copies = []
@@ -438,41 +427,39 @@
 
     for h in range(HEADS):
         arrive(ka_copies(3, h))
-        spread_rows(-row_total(3, h), ry, h)
-
-        def body(g, c):
-            sl = pl.ds(pl.multiple_of(g * 16, 16), 16)
-            zw = wide(ry[h, sl, :])
-            bb[sl, :] = (dd[h, sl, :] - kk[h, sl, :] * (zw * cv[h, SIGMA, 0:1, :])).astype(BF16)
+        spread_rows(-row_total(3, h), ra, h)
+
+        def body(cs, g, c):
+            sl = rows16(g)
+            low = strip_wide(ry[h, sl, :]) * cv[h, RHO, 0:1, cs] + cv[h, GAMMA, 0:1, cs]
+            low = low + strip_wide(ra[h, sl, :]) * cv[h, SIGMA, 0:1, cs]
+            bb[sl, cs] = (dd[h, sl, cs] - kk[h, sl, cs] * low).astype(BF16)
             return c
 
-        lax.fori_loop(0, rows // 16, body, 0, unroll=2)
+        strips(body)
         by_columns(qt, dk, h)
-        start(rs_first(1, h, dk))
-
-        def body(i, c):
-            sl = pl.ds(pl.multiple_of(i * mm, mm), mm)
-            res = jnp.dot(bb[sl, :], k[:, head(h)], preferred_element_type=F32)
-            for n in range(mm // LANES):
-                dq[h, i * (mm // LANES) + n] = res[n * LANES : (n + 1) * LANES]
-            return c
-
-        lax.fori_loop(0, rows // mm, body, 0)
+        rs_start(1, h, dk)
+        res = jnp.dot(bb[...], k[:, head(h)], preferred_element_type=F32)
+        for b in range(blocks):
+            dq[h, b] = res[b * LANES : (b + 1) * LANES]
         start(sq_copies(h))
-
-    for w, part in ((0, dv), (1, dk)):
-        for h in range(HEADS):
-            rs_middle(w, h, part)
-    for h in range(HEADS):
-        rs_last(0, h, 1.0, gv_ref)
-    for h in range(HEADS):
+        rs_middle(0, h, dv)
+
+    def query_last(h):
         arrive(sq_copies(h))
         total = dq[h, ka]
         for n in range(7):
             total = total + sq[h, n]
         gq_ref[:, head(h)] = total * HD**-0.5
-    for h in range(HEADS):
-        rs_last(1, h, HD**-0.5, gk_ref)
+
+    rs_middle(1, 0, dk)
+    rs_last(0, 0, 1.0, gv_ref)
+    query_last(0)
+    rs_middle(1, 1, dk)
+    rs_last(0, 1, 1.0, gv_ref)
+    rs_last(1, 0, HD**-0.5, gk_ref)
+    query_last(1)
+    rs_last(1, 1, HD**-0.5, gk_ref)
 
     for h in range(HEADS):
         for r in range(4):
@@ -480,9 +467,16 @@
         for r in range(3):
             drain(pb_copies(r, h))
         for w, part in ((0, dv), (1, dk)):
-            drain(rs_first(w, h, part))
-            drain(rs_second(w, h))
+            for e in range(2):
+                drain(rs_first(w, h, e, part))
+                drain(rs_second(w, h, e))
         drain(sq_copies(h))
+
+
+def settle(*refs):
+    count = len(refs) // 2
+    for n in range(count):
+        refs[count + n][...] = refs[n][...]
 
 
 def shards(queries, keys, values, grad_out, key_lengths):
@@ -502,15 +496,15 @@
         vmem(3, HEADS, 16, 2, cols // LANES, LANES),
         vmem(HEADS, 4, 4, HD, LANES), vmem(HEADS, 4, 4, HD, LANES),
         vmem(HEADS, rows // LANES, LANES, HD),
-        vmem(2, HEADS, 3, 4, HD, LANES), vmem(2, HEADS, 4, HD, LANES),
-        vmem(2, HEADS, 3, HD, LANES), vmem(HEADS, 7, LANES, HD),
+        vmem(2, HEADS, 2, 3, 4, HD // 2, LANES), vmem(2, HEADS, 2, 4, HD // 2, LANES),
+        vmem(2, HEADS, 2, 3, HD // 2, LANES), vmem(HEADS, 7, LANES, HD),
         dma(4), dma(4, HEADS, 7), dma(4, HEADS, 7), dma(3, HEADS, 15), dma(3, HEADS, 15),
-        dma(2, HEADS, 3), dma(2, HEADS, 3), dma(2, HEADS, 3), dma(2, HEADS, 3),
+        dma(2, HEADS, 2, 3), dma(2, HEADS, 2, 3), dma(2, HEADS, 2, 3), dma(2, HEADS, 2, 3),
         dma(HEADS, 7), dma(HEADS, 7),
     ]
     hbm = pl.BlockSpec(memory_space=pl.ANY)
     here = pl.BlockSpec(memory_space=pltpu.VMEM)
-    return pl.pallas_call(
+    results = pl.pallas_call(
         functools.partial(kernel, rows, cols),
         out_shape=(
             jax.ShapeDtypeStruct((rows // 8, width), F32),
@@ -527,6 +521,12 @@
             flops=24 * rows * cols * HD, bytes_accessed=2**22, transcendentals=4 * rows * cols
         ),
     )(key_lengths, queries, keys, values, grad_out)
+    return pl.pallas_call(
+        settle,
+        out_shape=tuple(jax.ShapeDtypeStruct(r.shape, F32) for r in results),
+        in_specs=[here] * 3,
+        out_specs=(here,) * 3,
+    )(*results)
 
 
 def solution(mesh):

time: 103 us -> 85.7 us (0.83)
  Pallas kernels: 98.8 us -> 83.8 us
  local copies, waits for them, and re-layouts: 3.21 us -> 0 us
    pallas_call x1, Pallas kernels: 98.8 us -> 82 us  [shards(): pl.pallas_call(functools.partial(kernel, rows, cols), out_shape=(jax.Shap...]
    unnamed x7 -> x0, local copies, waits for them, and re-layouts: 3.21 us -> none
    pallas_call x0 -> x1, Pallas kernels: none -> 1.78 us  [shards(): pl.pallas_call(settle, out_shape=tuple((jax.ShapeDtypeStruct(r.shape, F32...]
where the time goes in v2:
time: 85.7 us; the launch traced here: 85.1 us
  Pallas kernels  83.8 us (98%)
  between operations  1.29 us (2%)
    pallas_call x1, Pallas kernels, shards(): pl.pallas_call(functools.partial(kernel, rows, cols), out_shape=(jax.Shap...  82 us
    pallas_call x1, Pallas kernels, shards(): pl.pallas_call(settle, out_shape=tuple((jax.ShapeDtypeStruct(r.shape, F32...  1.78 us

profile of v2, /device:TPU:0, one launch (start us, length us, event | category | flops | bytes accessed | tf_op | source)
XLA Modules:
  0.0 85.1 jit_solution(10976787871882283399)
XLA Ops:
  1.3 82.0 %shard_map.76 = (f32[128,256]{1,0:T(8,128)}, f32[128,256]{1,0:T(8,128)}, f32[128,256]{1,0:T(8,128)}) custom-call(s32[1]{0:T(128)S(6)} %copy.8.len_ref, bf16[1024,256]{1,0:T(8,128)(2,1)} %q_hbm.1, bf16[2048,256]{1,0:T(8,128)(2,1)} %k_hbm.1, bf16[2048,256]{1,0:T(8,128)(2,1)} %v_hbm.1, bf16[1024,256]{1,0:T(8,128)(2,1)} %o_hbm.1), custom_call_target="tpu_custom_call" | custom-call | flops 6442450944 | bytes 4194304 | tf_op jit(solution)/shard_map/pallas_call | solution.py:507
  83.3 1.8 %shard_map.77 = (f32[128,256]{1,0:T(8,128)}, f32[128,256]{1,0:T(8,128)}, f32[128,256]{1,0:T(8,128)}) custom-call(f32[128,256]{1,0:T(8,128)} %get-tuple-element.6.refs_0_, f32[128,256]{1,0:T(8,128)} %get-tuple-element.7.refs_1_, f32[128,256]{1,0:T(8,128)} %get-tuple-element.8.refs_2_), custom_call_target="tpu_custom_call" | custom-call | tf_op jit(solution)/shard_map/pallas_call | solution.py:524

commit v3 on v2

--- a/solution.py
+++ b/solution.py
@@ -50,6 +50,9 @@
     def pb_peer(off):
         return (lax.rem(z + off[0], 4) * 4 + lax.rem(y + off[1], 4), ka)
 
+    ka_devs = [ka_peer(off) for off in KA_OFFS]
+    pb_devs = [pb_peer(off) for off in PB_OFFS]
+
     loads = [
         pltpu.make_async_copy(src, dst, in_sem.at[n])
         for n, (src, dst) in enumerate(((q_hbm, q), (k_hbm, k), (v_hbm, v), (o_hbm, o)))
@@ -57,19 +60,17 @@
     for copy in loads:
         copy.start()
     barrier = pltpu.get_barrier_semaphore()
-    for off in KA_OFFS:
-        pl.semaphore_signal(barrier, inc=1, device_id=ka_peer(off), device_id_type=MESH)
-    for off in PB_OFFS:
-        pl.semaphore_signal(barrier, inc=1, device_id=pb_peer(off), device_id_type=MESH)
+    for dev in pb_devs + ka_devs:
+        pl.semaphore_signal(barrier, inc=1, device_id=dev, device_id_type=MESH)
 
     def ka_copies(r, h):
         return [
             pltpu.make_async_remote_copy(
                 src_ref=kab.at[r, h, 0], dst_ref=kab.at[r, h, n + 1],
                 send_sem=ka_s.at[r, h, n], recv_sem=ka_r.at[r, h, n],
-                device_id=ka_peer(off), device_id_type=MESH,
+                device_id=dev, device_id_type=MESH,
             )
-            for n, off in enumerate(KA_OFFS)
+            for n, dev in enumerate(ka_devs)
         ]
 
     def pb_copies(r, h):
@@ -77,9 +78,9 @@
             pltpu.make_async_remote_copy(
                 src_ref=pbb.at[r, h, 0], dst_ref=pbb.at[r, h, n + 1],
                 send_sem=pb_s.at[r, h, n], recv_sem=pb_r.at[r, h, n],
-                device_id=pb_peer(off), device_id_type=MESH,
+                device_id=dev, device_id_type=MESH,
             )
-            for n, off in enumerate(PB_OFFS)
+            for n, dev in enumerate(pb_devs)
         ]
 
     def start(copies):
@@ -89,6 +90,13 @@
     def arrive(copies):
         for copy in copies:
             copy.wait_recv()
+
+    def each_head(step):
+        def body(h, c):
+            step(h)
+            return c
+
+        lax.fori_loop(0, HEADS, body, 0)
 
     def drain(copies):
         for copy in copies:
@@ -140,7 +148,7 @@
     spread_cols(jnp.where(valid, 0.0, NEG), BIAS, 0)
 
     def head(h):
-        return slice(h * HD, (h + 1) * HD)
+        return pl.ds(h * HD if isinstance(h, int) else pl.multiple_of(h * HD, HD), HD)
 
     def product(a, b, h):
         return lax.dot_general(
@@ -212,7 +220,8 @@
         pack_cols(peak, pbb.at[0, h, 0, 0])
         pack_cols(jnp.sum(acc, axis=0, keepdims=True), pbb.at[0, h, 0, 1])
 
-    for h in range(HEADS):
+    @each_head
+    def _(h):
         arrive(ka_copies(0, h))
         first_columns(h)
         start(pb_copies(0, h))
@@ -241,7 +250,8 @@
 
     loads[2].wait()
     loads[3].wait()
-    for h in range(HEADS):
+    @each_head
+    def _(h):
         output_product(h)
         arrive(pb_copies(0, h))
         logc = merge([(pbb[0, h, n, 0], pbb[0, h, n, 1]) for n in range(16)])
@@ -270,7 +280,8 @@
         pbb[1, h, 0, 0] = pbb[1, h, 0, 0] * kappa
         pbb[1, h, 0, 1] = pbb[1, h, 0, 1] * kappa
 
-    for h in range(HEADS):
+    @each_head
+    def _(h):
         arrive(ka_copies(1, h))
         second_columns(h)
         start(pb_copies(1, h))
@@ -294,7 +305,8 @@
         lax.fori_loop(0, groups, body, 0, unroll=4)
         pack_rows(2, h)
 
-    for h in range(HEADS):
+    @each_head
+    def _(h):
         arrive(pb_copies(1, h))
         second_rows(h)
         start(ka_copies(2, h))
@@ -405,7 +417,8 @@
     value_part(1)
     rs_start(0, 1, dv)
 
-    for h in range(HEADS):
+    @each_head
+    def _(h):
         arrive(pb_copies(2, h))
         adj = -jnp.exp2((1.0 - RELAX) * cp[h, LOGC]) * col_total(2, h, 0)
         spread_cols(RELAX * cp[h, KAPPA] * adj, GAMMA, h)
@@ -414,8 +427,7 @@
 
     def sq_copies(h):
         copies = []
-        for n, off in enumerate(KA_OFFS):
-            dev = ka_peer(off)
+        for n, dev in enumerate(ka_devs):
             copies.append(
                 pltpu.make_async_remote_copy(
                     src_ref=dq.at[h, dev[1]], dst_ref=sq.at[h, n],
@@ -425,7 +437,8 @@
             )
         return copies
 
-    for h in range(HEADS):
+    @each_head
+    def _(h):
         arrive(ka_copies(3, h))
         spread_rows(-row_total(3, h), ra, h)
 
@@ -443,7 +456,6 @@
         for b in range(blocks):
             dq[h, b] = res[b * LANES : (b + 1) * LANES]
         start(sq_copies(h))
-        rs_middle(0, h, dv)
 
     def query_last(h):
         arrive(sq_copies(h))
@@ -452,25 +464,33 @@
             total = total + sq[h, n]
         gq_ref[:, head(h)] = total * HD**-0.5
 
+    rs_middle(0, 0, dv)
+    rs_middle(0, 1, dv)
     rs_middle(1, 0, dk)
     rs_last(0, 0, 1.0, gv_ref)
     query_last(0)
-    rs_middle(1, 1, dk)
-    rs_last(0, 1, 1.0, gv_ref)
-    rs_last(1, 0, HD**-0.5, gk_ref)
-    query_last(1)
-    rs_last(1, 1, HD**-0.5, gk_ref)
-
     for h in range(HEADS):
         for r in range(4):
             drain(ka_copies(r, h))
         for r in range(3):
             drain(pb_copies(r, h))
-        for w, part in ((0, dv), (1, dk)):
+        for e in range(2):
+            drain(rs_first(0, h, e, dv))
+        drain(sq_copies(h))
+    for e in range(2):
+        drain(rs_first(1, 0, e, dk))
+    rs_middle(1, 1, dk)
+    for e in range(2):
+        drain(rs_first(1, 1, e, dk))
+    rs_last(0, 1, 1.0, gv_ref)
+    rs_last(1, 0, HD**-0.5, gk_ref)
+    query_last(1)
+    rs_last(1, 1, HD**-0.5, gk_ref)
+
+    for h in range(HEADS):
+        for w in range(2):
             for e in range(2):
-                drain(rs_first(w, h, e, part))
                 drain(rs_second(w, h, e))
-        drain(sq_copies(h))
 
 
 def settle(*refs):

time: 85.7 us -> 85 us (level)
  no operation moved by 1% of the time
where the time goes in v3:
time: 85 us; the launch traced here: 84.9 us
  Pallas kernels  83.6 us (98%)
  between operations  1.29 us (2%)
    pallas_call x1, Pallas kernels, shards(): pl.pallas_call(functools.partial(kernel, rows, cols), out_shape=(jax.Shap...  81.8 us
    pallas_call x1, Pallas kernels, shards(): pl.pallas_call(settle, out_shape=tuple((jax.ShapeDtypeStruct(r.shape, F32...  1.78 us

profile of v3, /device:TPU:0, one launch (start us, length us, event | category | flops | bytes accessed | tf_op | source)
XLA Modules:
  0.0 84.9 jit_solution(10320240578241527511)
XLA Ops:
  1.3 81.8 %shard_map.76 = (f32[128,256]{1,0:T(8,128)}, f32[128,256]{1,0:T(8,128)}, f32[128,256]{1,0:T(8,128)}) custom-call(s32[1]{0:T(128)S(6)} %copy.8.len_ref, bf16[1024,256]{1,0:T(8,128)(2,1)} %q_hbm.1, bf16[2048,256]{1,0:T(8,128)(2,1)} %k_hbm.1, bf16[2048,256]{1,0:T(8,128)(2,1)} %v_hbm.1, bf16[1024,256]{1,0:T(8,128)(2,1)} %o_hbm.1), custom_call_target="tpu_custom_call" | custom-call | flops 6442450944 | bytes 4194304 | tf_op jit(solution)/shard_map/pallas_call | solution.py:527
  83.1 1.8 %shard_map.77 = (f32[128,256]{1,0:T(8,128)}, f32[128,256]{1,0:T(8,128)}, f32[128,256]{1,0:T(8,128)}) custom-call(f32[128,256]{1,0:T(8,128)} %get-tuple-element.6.refs_0_, f32[128,256]{1,0:T(8,128)} %get-tuple-element.7.refs_1_, f32[128,256]{1,0:T(8,128)} %get-tuple-element.8.refs_2_), custom_call_target="tpu_custom_call" | custom-call | tf_op jit(solution)/shard_map/pallas_call | solution.py:544

commit v4 on v3

--- a/solution.py
+++ b/solution.py
@@ -347,8 +347,9 @@
         return copies
 
     def rs_start(w, h, part):
-        for e in range(2):
-            start(rs_first(w, h, e, part))
+        halves = [rs_first(w, h, e, part) for e in range(2)]
+        for pair in zip(*halves):
+            start(pair)
 
     def rs_middle(w, h, part):
         for e in range(2):

time: 85 us -> 85 us (level)
  no operation moved by 1% of the time
where the time goes in v4:
time: 85 us; the launch traced here: 84.9 us
  Pallas kernels  83.6 us (98%)
  between operations  1.29 us (2%)
    pallas_call x1, Pallas kernels, shards(): pl.pallas_call(functools.partial(kernel, rows, cols), out_shape=(jax.Shap...  81.8 us
    pallas_call x1, Pallas kernels, shards(): pl.pallas_call(settle, out_shape=tuple((jax.ShapeDtypeStruct(r.shape, F32...  1.78 us

profile of v4, /device:TPU:0, one launch (start us, length us, event | category | flops | bytes accessed | tf_op | source)
XLA Modules:
  0.0 84.9 jit_solution(15357373703967329182)
XLA Ops:
  1.3 81.8 %shard_map.76 = (f32[128,256]{1,0:T(8,128)}, f32[128,256]{1,0:T(8,128)}, f32[128,256]{1,0:T(8,128)}) custom-call(s32[1]{0:T(128)S(6)} %copy.8.len_ref, bf16[1024,256]{1,0:T(8,128)(2,1)} %q_hbm.1, bf16[2048,256]{1,0:T(8,128)(2,1)} %k_hbm.1, bf16[2048,256]{1,0:T(8,128)(2,1)} %v_hbm.1, bf16[1024,256]{1,0:T(8,128)(2,1)} %o_hbm.1), custom_call_target="tpu_custom_call" | custom-call | flops 6442450944 | bytes 4194304 | tf_op jit(solution)/shard_map/pallas_call | solution.py:528
  83.1 1.8 %shard_map.77 = (f32[128,256]{1,0:T(8,128)}, f32[128,256]{1,0:T(8,128)}, f32[128,256]{1,0:T(8,128)}) custom-call(f32[128,256]{1,0:T(8,128)} %get-tuple-element.6.refs_0_, f32[128,256]{1,0:T(8,128)} %get-tuple-element.7.refs_1_, f32[128,256]{1,0:T(8,128)} %get-tuple-element.8.refs_2_), custom_call_target="tpu_custom_call" | custom-call | tf_op jit(solution)/shard_map/pallas_call | solution.py:545
